TPU v7x, 512 devices: a whole 4x8x8 slice. The times are simulated.
512 devices in a mesh: rep: 16 (over x, y_lo), ep: 32 (over z, y_hi, core).
Axes of the slice: x: 4, y: 8 (y_hi: 2, y_lo: 4; y = y_hi * 4 + y_lo), z: 8, core: 2. Of those that a mesh axis runs over, the one named last changes fastest.
Arguments:
- cotangent: bfloat16 [65536, 1536], P(('rep', 'ep')), may hold values from -12 to 12
- expert_ids: int32 [65536, 4], P(('rep', 'ep')), may hold values from 0 to 31, all different within a row; in each aligned block of 128 rows (0 to 127, 128 to 255, ...) at most 32 rows name the same one
- route_weight: bfloat16 [65536, 4], P(('rep', 'ep')), may hold values from 0.049804688 to 0.59765625
- hidden: bfloat16 [16, 32, 32, 32, 1024], P('rep', 'ep'), may hold values from -0.119628906 to 0.119628906
- down_weight: bfloat16 [32, 1024, 1536], P('ep', 'rep'), may hold values from -0.1875 to 0.1875
Outputs:
- router_grad: float32 [65536, 4], P(('rep', 'ep'))
- hidden_grad: bfloat16 [16, 32, 32, 32, 1024], P('rep', 'ep')
- down_grad: bfloat16 [32, 1024, 1536], P('ep', 'rep')
Inputs may be any that keep to these rules, and one draw needn't show every extreme that they name: `expert_ids`: A token names 4 different experts; within the 128 tokens of one device no expert is named more than 32 times, and 32 is reached in some device.
All inputs are finite; a program needn't handle non-finite values.
Results may differ from a plain program's by a relative error of at most 0.022.
Values may be sent and summed in bfloat16 or wider, within the bound.
A program may use at most 64 MiB of HBM per device.

v0:
```python
import jax
import jax.numpy as jnp
from jax import lax
from jax.sharding import PartitionSpec as P


def on_device(cotangent, expert_ids, route_weight, hidden, down_weight):
    top_count = expert_ids.shape[1]
    capacity = hidden.shape[3]
    experts = down_weight.shape[0] * lax.axis_size("ep")
    flat_ids = expert_ids.reshape(-1)
    slot_total = flat_ids.shape[0]
    labels = jnp.arange(experts, dtype=jnp.int32)
    one_hot = (flat_ids[:, None] == labels[None, :]).astype(jnp.int32)
    slot_rank = jnp.sum((jnp.cumsum(one_hot, axis=0) - one_hot) * one_hot, axis=1)
    destination = flat_ids * capacity + slot_rank
    marker = jnp.zeros((experts * capacity,), jnp.int32)
    marker = marker.at[destination].set(jnp.arange(1, slot_total + 1, dtype=jnp.int32))
    filled = marker > 0
    slot_index = jnp.maximum(marker - 1, 0)
    token_rows = cotangent[slot_index // top_count]
    send_rows = jnp.where(filled[:, None], token_rows, jnp.zeros_like(token_rows))
    send_rows = send_rows.reshape(experts, capacity, cotangent.shape[1])
    slot_weight = route_weight.reshape(-1)[slot_index]
    send_weight = jnp.where(filled, slot_weight, jnp.zeros_like(slot_weight)).reshape(
        experts, capacity
    )
    sources = lax.axis_size("ep")
    width = cotangent.shape[1]
    saved = hidden.reshape(sources * capacity, hidden.shape[4])
    own_weight = down_weight[0]
    contract_last = (((1,), (1,)), ((), ()))
    routed, routed_weight = (
        lax.all_to_all(send_rows, "ep", split_axis=0, concat_axis=0, tiled=True),
        lax.all_to_all(send_weight, "ep", split_axis=0, concat_axis=0, tiled=True),
    )
    routed_rows = routed.reshape(sources * capacity, width)
    weight_column = routed_weight.reshape(-1).astype(jnp.float32)
    gathered = lax.all_gather(own_weight, "rep", axis=0, tiled=True)
    backward = lax.dot_general(
        routed_rows, gathered, contract_last, preferred_element_type=jnp.float32
    )
    weighted = (weight_column[:, None] * routed_rows.astype(jnp.float32)).astype(jnp.bfloat16)
    down_grad = lax.psum_scatter(
        lax.dot_general(
            saved, weighted, (((0,), (0,)), ((), ())), preferred_element_type=jnp.float32
        ).astype(jnp.bfloat16),
        "rep",
        scatter_dimension=0,
        tiled=True,
    )
    hidden_grad = (weight_column[:, None] * backward).astype(jnp.bfloat16).reshape(hidden.shape)
    score = jnp.sum(saved.astype(jnp.float32) * backward, axis=1).reshape(sources, capacity)
    returned = lax.all_to_all(score, "ep", split_axis=0, concat_axis=0, tiled=True)
    router_grad = returned.reshape(-1)[destination].reshape(expert_ids.shape)
    return (router_grad, hidden_grad, down_grad[None])


def solution(mesh):
    in_specs = (
        P(("rep", "ep"), None),
        P(("rep", "ep"), None),
        P(("rep", "ep"), None),
        P("rep", "ep", None, None, None),
        P("ep", "rep", None),
    )
    out_specs = (P(("rep", "ep"), None), P("rep", "ep", None, None, None), P("ep", "rep", None))
    return jax.shard_map(
        on_device, mesh=mesh, in_specs=in_specs, out_specs=out_specs, check_vma=False
    )
```

profile of v0, /device:TPU:64, one launch (start us, length us, event | category | flops | bytes accessed | tf_op | source)
XLA Modules:
  0.0 324.2 jit_solution(13623880665875475892)
XLA Ops:
  7.2 0.0 copy-start
  7.2 0.8 copy.24
  8.0 0.1 eq.29
  8.1 0.1 eq.25
  8.2 0.7 broadcast_multiply_fusion
  8.9 1.2 reduce-window.6
  10.1 0.2 slice_reduce_fusion
  10.4 0.1 copy.23
  10.5 0.1 mul.41
  10.6 0.1 fusion.5
  10.7 2.4 scatter_custom_fusion
  13.2 0.6 fusion.9
  13.8 0.8 copy.27
  14.6 0.1 reshape.110
  14.7 6.8 %gather_fusion.2 = bf16[1024]{0:T(1024)(128)(2,1)S(1)} fusion(bf16[512]{0:T(512)(128)(2,1)S(1)} %reshape.110, s32[1024]{0:T(1024)S(1)} %get-tuple-element.19), kind=kCustom, calls=%fused_computation.2 | custom fusion | bytes 8192 | tf_op jit(solution)/shard_map/gather | solution.py:24
  21.5 0.7 all_to_all.20
  22.2 15.4 %all-to-all-start.2 = ((bf16[32,1,32]{2,1,0:T(2,128)(2,1)}), bf16[32,1,32]{2,1,0:T(2,128)(2,1)S(1)}, u32[]{:S(2)}, u32[]{:S(2)}) async-start(bf16[32,1,32]{2,1,0:T(2,128)(2,1)} %all_to_all.20), calls=%async_computation.2 | async-start | bytes 32768 | tf_op jit(solution)/shard_map/all_to_all | solution.py:35
  37.6 0.7 broadcast_in_dim.31
  38.3 4.6 %gather_fusion = bf16[1024,1536]{1,0:T(8,128)(2,1)S(1)} fusion(bf16[128,1536]{1,0:T(8,128)(2,1)S(1)} %copy-done, s32[1024]{0:T(1024)} %get-tuple-element.20), kind=kCustom, calls=%fused_computation | custom fusion | bytes 6295552 | tf_op jit(solution)/shard_map/gather | solution.py:21
  42.9 2.7 broadcast_select_fusion
  45.6 2.9 all-to-all-done.2
  48.5 9.3 %all-to-all-start = ((bf16[32,32,1536]{2,1,0:T(8,128)(2,1)}), bf16[32,32,1536]{2,1,0:T(8,128)(2,1)S(1)}, u32[]{:S(2)}, u32[]{:S(2)}) async-start(bf16[32,32,1536]{2,1,0:T(8,128)(2,1)} %broadcast_select_fusion), calls=%async_computation | async-start | bytes 6291456 | tf_op jit(solution)/shard_map/all_to_all | solution.py:34
  57.8 0.0 all-gather.3.cloned.1.call-start
  57.9 0.7 all-gather.3.cloned.1.call-update
  58.5 0.0 reduce-scatter.4.cloned.1.call-start
  58.6 0.6 convert_element_type.58
  59.2 84.7 %all-to-all-done = bf16[32,32,1536]{2,1,0:T(8,128)(2,1)S(1)} async-done(((bf16[32,32,1536]{2,1,0:T(8,128)(2,1)}), bf16[32,32,1536]{2,1,0:T(8,128)(2,1)S(1)}, u32[]{:S(2)}, u32[]{:S(2)}) %all-to-all-start) | async-done | bytes 3145760 | tf_op jit(solution)/shard_map/all_to_all | solution.py:34
  144.0 1.4 multiply_convert_fusion
  145.4 0.2 copy-done.3
  145.6 4.9 %fusion = bf16[1024,1536]{0,1:T(8,128)(2,1)} fusion(bf16[1024,1536]{1,0:T(8,128)(2,1)S(1)} %bitcast.42, bf16[1024,1024]{1,0:T(8,128)(2,1)S(1)} %bitcast.48), kind=kOutput, calls=%fused_computation.8 | convolution fusion | flops 3222798336 | bytes 8388608 | tf_op jit(solution)/shard_map/dot_general | solution.py:45
  150.5 4.7 %copy.31 = bf16[1024,1536]{1,0:T(8,128)(2,1)} copy(bf16[1024,1536]{0,1:T(8,128)(2,1)} %fusion) | data formatting | bytes 6291456
  155.2 0.0 reduce-scatter.4.cloned.1.call-update
  155.2 0.7 convert_reduce_fusion
  155.9 0.8 reshape.112
  156.7 42.3 %all-gather.3.cloned.1.call-done = bf16[1,1024,1536]{2,1,0:T(8,128)(2,1)} async-done(((bf16[1,64,1536]{2,1,0:T(8,128)(2,1)}), bf16[1,1024,1536]{2,1,0:T(8,128)(2,1)}) %all-gather.3.cloned.1.call-update) | async-done | bytes 3145744 | tf_op jit(solution)/shard_map/all_gather | solution.py:39
  199.0 7.0 %multiply_convert_fusion.1 = (bf16[1024,1024]{1,0:T(8,128)(2,1)}, f32[1024]{0:T(1024)S(1)}) fusion(f32[1024]{0:T(1024)S(1)} %reshape.112, bf16[1,1,32,32,1024]{4,3,2,1,0:T(8,128)(2,1)} %param.8, bf16[1024,1536]{1,0:T(8,128)(2,1)S(1)} %bitcast.40, bf16[1,1024,1536]{2,1,0:T(8,128)(2,1)} %all-gather.3.cloned.1.call-done), kind=kOutput, calls=%fused_computation.5 | convolution fusion | flops 3226467328 | bytes 10493952 | tf_op jit(solution)/shard_map/dot_general | solution.py:40
  206.0 0.7 all_to_all.16
  206.6 20.2 %all-to-all-start.1 = ((f32[32,1,32]{2,1,0:T(1,128)}), f32[32,1,32]{2,1,0:T(1,128)S(1)}, u32[]{:S(2)}, u32[]{:S(2)}) async-start(f32[32,1,32]{2,1,0:T(1,128)} %all_to_all.16), calls=%async_computation.1 | async-start | bytes 32768 | tf_op jit(solution)/shard_map/all_to_all | solution.py:54
  226.9 10.9 %all-to-all-done.1 = f32[32,1,32]{2,1,0:T(1,128)S(1)} async-done(((f32[32,1,32]{2,1,0:T(1,128)}), f32[32,1,32]{2,1,0:T(1,128)S(1)}, u32[]{:S(2)}, u32[]{:S(2)}) %all-to-all-start.1) | async-done | bytes 4128 | tf_op jit(solution)/shard_map/all_to_all | solution.py:54
  237.8 0.5 broadcast.98
  238.3 0.7 reduce.9
  239.0 0.1 reshape.108
  239.0 2.3 gather_fusion.1
  241.3 0.1 reshape.109
  241.4 0.7 copy.29
  242.1 73.2 %reduce-scatter.4.cloned.1.call-done = bf16[64,1536]{1,0:T(8,128)(2,1)} async-done(((bf16[1024,1536]{1,0:T(8,128)(2,1)}), bf16[64,1536]{1,0:T(8,128)(2,1)}) %reduce-scatter.4.cloned.1.call-update) | async-done | bytes 196624
  315.3 1.1 copy.32
  316.5 0.8 copy.30
  (13 shorter events, 0.1 us)
Async XLA Ops:
  7.2 31.1 %copy-start = (bf16[128,1536]{1,0:T(8,128)(2,1)S(1)}, bf16[128,1536]{1,0:T(8,128)(2,1)}, u32[]{:S(2)}) copy-start(bf16[128,1536]{1,0:T(8,128)(2,1)} %param.5) | copy-start | bytes 1179652
  10.7 3.1 copy-start.1
  22.2 26.3 %all-to-all-start.2 = ((bf16[32,1,32]{2,1,0:T(2,128)(2,1)}), bf16[32,1,32]{2,1,0:T(2,128)(2,1)S(1)}, u32[]{:S(2)}, u32[]{:S(2)}) async-start(bf16[32,1,32]{2,1,0:T(2,128)(2,1)} %all_to_all.20), calls=%async_computation.2 | async-start | bytes 32768 | tf_op jit(solution)/shard_map/all_to_all | solution.py:35
  48.5 95.4 %all-to-all-start = ((bf16[32,32,1536]{2,1,0:T(8,128)(2,1)}), bf16[32,32,1536]{2,1,0:T(8,128)(2,1)S(1)}, u32[]{:S(2)}, u32[]{:S(2)}) async-start(bf16[32,32,1536]{2,1,0:T(8,128)(2,1)} %broadcast_select_fusion), calls=%async_computation | async-start | bytes 6291456 | tf_op jit(solution)/shard_map/all_to_all | solution.py:34
  57.8 141.1 %all-gather.3.cloned.1.call-start = ((), (), s32[]{:S(2)}) async-start(), calls=%async_computation.4 | async-start | bytes 3342336 | tf_op jit(solution)/shard_map/all_gather | solution.py:39
  58.5 256.8 %reduce-scatter.4.cloned.1.call-start = ((), (), s32[]{:S(2)}) async-start(), calls=%async_computation.5 | async-start | bytes 3342336
  144.0 1.6 copy-start.3
  199.0 27.9 %copy-start.2 = (s32[512,1]{0,1:T(1,128)S(1)}, s32[512,1]{0,1:T(1,128)}, u32[]{:S(2)}) copy-start(s32[512,1]{0,1:T(1,128)} %copy-done.1) | copy-start | bytes 6148
  206.6 31.1 %all-to-all-start.1 = ((f32[32,1,32]{2,1,0:T(1,128)}), f32[32,1,32]{2,1,0:T(1,128)S(1)}, u32[]{:S(2)}, u32[]{:S(2)}) async-start(f32[32,1,32]{2,1,0:T(1,128)} %all_to_all.16), calls=%async_computation.1 | async-start | bytes 32768 | tf_op jit(solution)/shard_map/all_to_all | solution.py:54
Sparse Core Ops, SparseCore 0:
  60.7 138.1 all-gather.2
  201.8 113.4 reduce-scatter.3
where the time goes:
time: 325 us; the launch traced here: 324 us
  waiting for transfers between devices  215 us (66%)
  starting transfers between devices  45 us (14%)
  local copies, waits for them, and re-layouts  29.6 us (9%)
  between operations  14.2 us (4%)
  matrix products  11.9 us (4%)
  other arithmetic  8.71 us (3%)
    all_to_all x1, waiting for transfers between devices, on_device(): lax.all_to_all(send_rows, 'ep', split_axis=0, concat_axis=0, tiled=True)  84.7 us
    unnamed x3, waiting for transfers between devices  73.9 us
    all_gather x1, waiting for transfers between devices, on_device(): gathered = lax.all_gather(own_weight, 'rep', axis=0, tiled=True)  42.3 us
    all_to_all x1, starting transfers between devices, on_device(): lax.all_to_all(score, 'ep', split_axis=0, concat_axis=0, tiled=True)  20.2 us
    all_to_all x1, starting transfers between devices, on_device(): lax.all_to_all(send_weight, 'ep', split_axis=0, concat_axis=0, tiled=True)  15.4 us
    all_to_all x1, waiting for transfers between devices, on_device(): lax.all_to_all(score, 'ep', split_axis=0, concat_axis=0, tiled=True)  10.9 us
    all_to_all x1, starting transfers between devices, on_device(): lax.all_to_all(send_rows, 'ep', split_axis=0, concat_axis=0, tiled=True)  9.29 us
    unnamed x14, local copies, waits for them, and re-layouts  9.16 us
  transfers between devices with their start and end apart: 5, of which 5 were waited for; matrix products, arithmetic and copies ran while one was open for 10% of the time, Pallas kernels for 0%

commit v1 on v0

v1 whole, which is shorter than its diff:
```python
import functools

import jax
import jax.numpy as jnp
from jax import lax
from jax.experimental import pallas as pl
from jax.experimental.pallas import tpu as pltpu
from jax.sharding import PartitionSpec as P

MESH = pl.DeviceIdType.MESH
BF, F32 = jnp.bfloat16, jnp.float32
NT = (((1,), (1,)), ((), ()))
CHUNKS = 4


def remote(src, dst, send, recv, device):
    return pltpu.make_async_remote_copy(
        src_ref=src, dst_ref=dst, send_sem=send, recv_sem=recv, device_id=device, device_id_type=MESH
    )


def kernel(
    ct, ids, rw, hid_in, dw, rg, hg_out, dg_out,
    G, MT, PP, WR, WS, S, R, WB, hid, hidT, WG, back, PB, TA, TB, OWN, XH, XF, YB, YO, YR, DG, HG,
    SCB, L1, TT, L2, CODE,
    ld, out_sem, ms, mr, ys, yr, zs, zr, cs, cr, wys, wyr, wxs, wxr, xhs, xhr, xfs, xfr, yls, ylr,
    s1s, s1r, s2s, s2r,
):
    nc = G.shape[2]
    W = G.shape[4]
    rep, ep = lax.axis_index("rep"), lax.axis_index("ep")
    x, yl = rep // 4, rep % 4
    z, h, core = ep // 4, (ep // 2) % 2, ep % 2
    other = 1 - core
    ph = 1 - h

    def z_dev(k):
        return (rep, ((z + k + 8) % 8) * 4 + h * 2 + core)

    def x_dev(k):
        return (((x + k + 4) % 4) * 4 + yl, ep)

    def yl_dev(k):
        return (x * 4 + (yl + k) % 4, ep)

    def hc_dev(m):
        hh = ph if m // 2 else h
        cc = other if m % 2 else core
        return (rep, z * 4 + hh * 2 + cc)

    core_dev, y_dev = hc_dev(1), hc_dev(2)

    loads = []
    for c in range(nc):
        loads.append(pltpu.make_async_copy(ct.at[:, pl.ds(c * W, W)], G.at[z, h, c], ld.at[c]))
    w_loads = []
    for c in range(nc):
        w_loads.append(pltpu.make_async_copy(dw.at[:, pl.ds(c * W, W)], WG.at[c, rep], ld.at[nc + c]))
    h_loads = []
    for k in range(4):
        h_loads.append(pltpu.make_async_copy(hid_in.at[:, k // 2, k % 2], hid.at[:, k % 2, k // 2], ld.at[2 * nc + k]))
    for cp in loads + w_loads + h_loads:
        cp.start()

    peers = [z_dev(k) for k in range(1, 8)] + [x_dev(1), x_dev(-1)] + [yl_dev(k) for k in (1, 2, 3)] + [hc_dev(m) for m in (1, 2, 3)]
    barrier = pltpu.get_barrier_semaphore()
    for p in peers:
        pl.semaphore_signal(barrier, inc=1, device_id=p, device_id_type=MESH)

    idf = ids[...].astype(F32)
    wf = rw[...].astype(F32)
    lane_e = lax.broadcasted_iota(jnp.int32, (128, 128), 1).astype(F32)
    sub_t = lax.broadcasted_iota(jnp.int32, (128, 128), 0).astype(F32)
    named = jnp.zeros((128, 128), F32)
    for k in range(4):
        named = named + jnp.where(idf[:, k : k + 1] == lane_e, 1.0, 0.0)
    before = jnp.where(sub_t > lane_e, 1.0, 0.0)
    count = jnp.dot(before.astype(BF), named.astype(BF), preferred_element_type=F32)
    packed = jnp.zeros((128, 128), F32)
    for k in range(4):
        own = idf[:, k : k + 1]
        rank = jnp.sum(jnp.where(own == lane_e, count, 0.0), axis=1, keepdims=True)
        packed = jnp.where(lane_e == k, own * 32.0 + rank, packed)
        packed = jnp.where(lane_e == 4 + k, wf[:, k : k + 1], packed)
        packed = jnp.where(lane_e == 8 + k, rank, packed)
    CODE[...] = packed
    MT[z, h] = packed.T[0:8, :]

    pl.semaphore_wait(barrier, len(peers))

    def meta_y():
        return remote(MT.at[z, h], MT.at[z, h], ms.at[0], mr.at[0], y_dev)

    def meta_y_in():
        return remote(MT.at[z, ph], MT.at[z, ph], ms.at[0], mr.at[0], y_dev)

    def meta_z(k):
        return remote(MT.at[z], MT.at[z], ms.at[k], mr.at[k], z_dev(k))

    def meta_z_in(k):
        o = (z - k + 8) % 8
        return remote(MT.at[o], MT.at[o], ms.at[k], mr.at[k], z_dev(-k))

    def tok_y(c):
        return remote(G.at[z, h, c], G.at[z, h, c], ys.at[c], yr.at[c], y_dev)

    def tok_y_in(c):
        return remote(G.at[z, ph, c], G.at[z, ph, c], ys.at[c], yr.at[c], y_dev)

    def far(way, d):
        return (z - d + 8) % 8 if way == 0 else (z + d) % 8

    def hi(which):
        return h if which == 0 else ph

    def tok_z(c, which, way, s):
        blk = G.at[far(way, s), hi(which), c]
        return remote(blk, blk, zs.at[c, which, way, s], zr.at[c, which, way, s], z_dev(1 if way == 0 else -1))

    def tok_z_in(c, which, way, s):
        blk = G.at[far(way, s + 1), hi(which), c]
        return remote(blk, blk, zs.at[c, which, way, s], zr.at[c, which, way, s], z_dev(-1 if way == 0 else 1))

    def sends(s):
        return [(0, 0), (0, 1), (1, 0), (1, 1)] if s < 3 else [(0, 0), (1, 1)]

    def swap(c):
        return remote(S.at[c], R.at[c, :, core], cs.at[c], cr.at[c], core_dev)

    def swap_in(c):
        return remote(S.at[c], R.at[c, :, other], cs.at[c], cr.at[c], core_dev)

    def swap_w():
        return remote(WS, WR.at[:, core], cs.at[nc], cr.at[nc], core_dev)

    def swap_w_in():
        return remote(WS, WR.at[:, other], cs.at[nc], cr.at[nc], core_dev)

    def w_y(k):
        return remote(WG.at[:, rep], WG.at[:, rep], wys.at[k - 1], wyr.at[k - 1], yl_dev(k))

    def w_y_in(k):
        o = x * 4 + (yl - k + 4) % 4
        return remote(WG.at[:, o], WG.at[:, o], wys.at[k - 1], wyr.at[k - 1], yl_dev(-k + 4))

    def w_x(way):
        blk = WG.at[:, pl.ds(x * 4, 4)]
        return remote(blk, blk, wxs.at[way], wxr.at[way], x_dev(1 if way == 0 else -1))

    def w_x_in(way):
        o = (x - 1 + 4) % 4 if way == 0 else (x + 1) % 4
        blk = WG.at[:, pl.ds(o * 4, 4)]
        return remote(blk, blk, wxs.at[way], wxr.at[way], x_dev(-1 if way == 0 else 1))

    def w_half(way):
        o = (x - 1 + 4) % 4 if way == 0 else (x + 1) % 4
        blk = WG.at[:, pl.ds(o * 4 + 2 * way, 2)]
        return remote(blk, blk, wxs.at[2 + way], wxr.at[2 + way], x_dev(1 if way == 0 else -1))

    def w_half_in(way):
        o = (x + 2) % 4
        blk = WG.at[:, pl.ds(o * 4 + 2 * way, 2)]
        return remote(blk, blk, wxs.at[2 + way], wxr.at[2 + way], x_dev(-1 if way == 0 else 1))

    x_two, x_up, x_down = (x + 2) % 4, (x + 1) % 4, (x + 3) % 4

    def x_half(c, side):
        return remote(PB.at[c, x_two, side], XH.at[c, side], xhs.at[c, side], xhr.at[c, side], x_dev(-1 if side == 0 else 1))

    def x_full(c, side):
        return remote(PB.at[c, x_down if side == 0 else x_up], XF.at[c, side], xfs.at[c, side], xfr.at[c, side], x_dev(-1 if side == 0 else 1))

    def y_part(c, k):
        return remote(YB.at[c, (yl + k) % 4], YR.at[c, k - 1], yls.at[c, k - 1], ylr.at[c, k - 1], yl_dev(k))

    def score_z(k):
        return remote(SCB.at[(z + k) % 8], L1.at[z], s1s.at[k - 1], s1r.at[k - 1], z_dev(k))

    def score_z_in(k):
        o = (z - k + 8) % 8
        return remote(SCB.at[o], L1.at[o], s1s.at[k - 1], s1r.at[k - 1], z_dev(-k))

    def score_hc(m):
        mine = h * 2 + core
        return remote(TT, L2.at[mine], s2s.at[m - 1], s2r.at[m - 1], hc_dev(m))

    def score_hc_in(m):
        theirs = (ph if m // 2 else h) * 2 + (other if m % 2 else core)
        return remote(TT, L2.at[theirs], s2s.at[m - 1], s2r.at[m - 1], hc_dev(m))

    meta_y().start()
    for c in range(nc):
        loads[c].wait()
        if c == 0:
            tok_y(0).start()
            for way in (0, 1):
                tok_z(0, 0, way, 0).start()
    for c in range(nc):
        w_loads[c].wait()
    for k in (1, 2, 3):
        w_y(k).start()
    meta_y_in().wait_recv()
    for k in range(1, 8):
        meta_z(k).start()

    for k in range(4):
        h_loads[k].wait()

    def turn(q, _):
        blk = hid[q].reshape(128, 1024)
        hidT[q] = blk.T
        return 0

    lax.fori_loop(0, 8, turn, 0)

    def clear(q, _):
        back[q] = jnp.zeros((256, 1024), F32)
        return 0

    lax.fori_loop(0, 4, clear, 0)

    for k in range(1, 8):
        meta_z_in(k).wait_recv()
    expert = (ep * 32).astype(F32)
    expert_other = ((z * 4 + h * 2 + other) * 32).astype(F32)

    def select(n, _):
        zz, hh = n // 2, n % 2
        m = MT[zz, hh]
        row = lax.broadcasted_iota(jnp.int32, (64, 128), 0).astype(F32)
        target = jnp.where(row < 32.0, row + expert, row - 32.0 + expert_other)
        pick = jnp.zeros((64, 128), F32)
        weight = jnp.zeros((64, 128), F32)
        for k in range(4):
            same = m[k : k + 1, :] == target
            pick = jnp.where(same, 1.0, pick)
            weight = jnp.where(same, m[4 + k : 5 + k, :], weight)
        PP[zz, hh] = pick.astype(BF)
        wide = jnp.dot(weight.astype(BF), jnp.ones((128, 128), BF), preferred_element_type=F32).astype(BF)
        WR[zz, core, hh] = wide[0:32]
        WS[zz, hh] = wide[32:64]
        return 0

    lax.fori_loop(0, 16, select, 0)
    swap_w().start()
    swap_w_in().wait_recv()

    def pack(c, zz, hh):
        rows = jnp.dot(PP[zz, hh], G[zz, hh, c], preferred_element_type=F32).astype(BF)
        R[c, zz, core, hh] = rows[0:32]
        S[c, zz, hh] = rows[32:64]

    def forward(c, s):
        for which in (0, 1):
            for way in (0, 1):
                tok_z_in(c, which, way, s - 1).wait_recv()
                if (which, way) in sends(s):
                    tok_z(c, which, way, s).start()

    def pack_far(c, d):
        for which in (0, 1):
            for way in (0, 1):
                pack(c, far(way, d), hi(which))

    def partial(q):
        total = jnp.zeros((256, W), F32)
        for n in range(8):
            total = total + jnp.dot(hidT[n, pl.ds(q * 256, 256)], WB[n], preferred_element_type=F32)
        return total

    def backward(c):
        def rows(q, _):
            r = R[c, pl.ds(q * 2, 2)].reshape(256, W)
            w = WG[c].reshape(1024, W)
            back[q] = back[q] + lax.dot_general(r, w, NT, preferred_element_type=F32)
            return 0

        lax.fori_loop(0, 4, rows, 0)

    def weigh(c):
        def block(n, _):
            wide = WR[n].reshape(128, 128).astype(F32)
            wide = jnp.concatenate([wide] * (W // 128), axis=1)
            WB[n] = (R[c, n].reshape(128, W).astype(F32) * wide).astype(BF)
            return 0

        lax.fori_loop(0, 8, block, 0)

    def turn_of(i, _):
        gather = i < nc
        more = i + 1 < nc
        work = (i >= 1) & (i <= nc)
        a, b, d, f = i, i - 1, i - 2, i - 3

        @pl.when(gather)
        def _():
            tok_y_in(a).wait_recv()
            for way in (0, 1):
                tok_z(a, 1, way, 0).start()

        @pl.when(more)
        def _():
            tok_y(a + 1).start()

        @pl.when(work)
        def _():
            for which, way in sends(3):
                tok_z_in(b, which, way, 3).wait_recv()
            pack(b, (z + 4) % 8, h)
            pack(b, (z + 4) % 8, ph)
            swap(b).start()

        @pl.when(gather)
        def _():
            pack(a, z, h)
            pack(a, z, ph)
            forward(a, 1)
            pack_far(a, 1)

        @pl.when(work)
        def _():
            swap_in(b).wait_recv()
            weigh(b)
            PB[b, x_two] = partial(x_two).astype(BF).reshape(2, 128, W)
            x_half(b, 0).start()
            x_half(b, 1).start()

        @pl.when(gather)
        def _():
            forward(a, 2)

        @pl.when(more)
        def _():
            for way in (0, 1):
                tok_z(a + 1, 0, way, 0).start()

        @pl.when(gather)
        def _():
            pack_far(a, 2)

        @pl.when(i == 0)
        def _():
            for k in (1, 2, 3):
                w_y_in(k).wait_recv()
            w_x(0).start()
            w_x(1).start()

        @pl.when(i == 1)
        def _():
            for way in (0, 1):
                w_x_in(way).wait_recv()
                w_half(way).start()

        @pl.when(i == 2)
        def _():
            for way in (0, 1):
                w_half_in(way).wait_recv()

        @pl.when(work)
        def _():
            TA[...] = partial(x_down)
            TB[...] = partial(x_up)
            OWN[b] = partial(x)
            x_half(b, 0).wait_recv()
            PB[b, x_down, 0] = (TA[0:128] + XH[b, 0].astype(F32)).astype(BF)
            PB[b, x_down, 1] = TA[128:256].astype(BF)
            x_full(b, 0).start()
            x_half(b, 1).wait_recv()
            PB[b, x_up, 0] = TB[0:128].astype(BF)
            PB[b, x_up, 1] = (TB[128:256] + XH[b, 1].astype(F32)).astype(BF)
            x_full(b, 1).start()

        @pl.when(gather)
        def _():
            forward(a, 3)
            pack_far(a, 3)

        @pl.when((i >= 2) & (i <= nc + 1))
        def _():
            x_full(d, 0).wait_recv()
            x_full(d, 1).wait_recv()
            got = XF[d, 0].reshape(256, W).astype(F32) + XF[d, 1].reshape(256, W).astype(F32)
            OWN[d] = OWN[d] + got
            YB[d] = OWN[d].reshape(4, 64, W).astype(BF)
            YO[d] = OWN[d, pl.ds(yl * 64, 64)]
            for k in (1, 2, 3):
                y_part(d, k).start()

        @pl.when((i >= 2) & (i <= nc))
        def _():
            backward(d)

        @pl.when(i == nc)
        def _():
            backward(b)

            def finish(q, _):
                def half(u, _):
                    t = back[q, pl.ds(u * 128, 128)]
                    n = q * 2 + u
                    wide = WR[n].reshape(128, 128).astype(F32)
                    wide = jnp.concatenate([wide] * 8, axis=1)
                    HG[n] = (wide * t).astype(BF).reshape(2, 2, 32, 1024)
                    col = jnp.sum(hid[n].reshape(128, 1024).astype(F32) * t, axis=1, keepdims=True)
                    SCB[n] = jnp.broadcast_to(col, (128, 128)).T[0:8, :]
                    return 0

                lax.fori_loop(0, 2, half, 0)
                return 0

            lax.fori_loop(0, 4, finish, 0)
            for k in range(4):
                pltpu.make_async_copy(HG.at[:, k % 2, k // 2], hg_out.at[:, k // 2, k % 2], out_sem.at[k]).start()
            for k in range(1, 8):
                score_z(k).start()
            L1[z] = SCB[z]

        @pl.when(i == nc + 1)
        def _():
            for k in range(1, 8):
                score_z_in(k).wait_recv()
            sub = lax.broadcasted_iota(jnp.int32, (8, 128), 0)
            tile = jnp.zeros((8, 128), F32)
            for n in range(8):
                tile = jnp.where(sub == n, L1[n], tile)
            TT[...] = tile
            for m in (1, 2, 3):
                score_hc(m).start()
            L2[h * 2 + core] = tile

        @pl.when(i >= 3)
        def _():
            total = YO[f]
            for k in (1, 2, 3):
                y_part(f, k).wait_recv()
                total = total + YR[f, k - 1].astype(F32)
            DG[f] = total.astype(BF)
            pltpu.make_async_copy(DG.at[f], dg_out.at[:, pl.ds(pl.multiple_of(f * W, 128), W)], out_sem.at[4 + f]).start()

        return 0

    lax.fori_loop(0, nc + 3, turn_of, 0)

    for m in (1, 2, 3):
        score_hc_in(m).wait_recv()
    value = L2[...].reshape(32, 128)
    lane32 = lax.broadcasted_iota(jnp.int32, (128, 32), 1)
    order = ((lane32 % 8) * 4 + lane32 // 8).astype(F32)
    lane = lax.broadcasted_iota(jnp.int32, (128, 128), 1).astype(F32)
    mine = ((core * 2 + h) * 32).astype(F32)
    code = CODE[...]
    result = jnp.zeros((128, 128), F32)
    for k in range(4):
        hot = jnp.where(ids[:, k : k + 1].astype(F32) == order, 1.0, 0.0)
        row = jnp.dot(hot, value, preferred_element_type=F32, precision=lax.Precision.HIGHEST)
        got = jnp.sum(jnp.where(lane == mine + code[:, 8 + k : 9 + k], row, 0.0), axis=1, keepdims=True)
        result = jnp.where(lane == k, got, result)
    rg[...] = result[:, 0:4]

    meta_y().wait_send()
    for k in range(1, 8):
        meta_z(k).wait_send()
        score_z(k).wait_send()
    for m in (1, 2, 3):
        score_hc(m).wait_send()
        w_y(m).wait_send()
    for way in (0, 1):
        w_x(way).wait_send()
        w_half(way).wait_send()
    swap_w().wait_send()

    def drain(c, _):
        tok_y(c).wait_send()
        for s in range(4):
            for which, way in sends(s):
                tok_z(c, which, way, s).wait_send()
        swap(c).wait_send()
        for side in (0, 1):
            x_half(c, side).wait_send()
            x_full(c, side).wait_send()
        for k in (1, 2, 3):
            y_part(c, k).wait_send()
        pltpu.make_async_copy(DG.at[c], dg_out.at[:, pl.ds(pl.multiple_of(c * W, 128), W)], out_sem.at[4 + c]).wait()
        return 0

    lax.fori_loop(0, nc, drain, 0)
    for k in range(4):
        pltpu.make_async_copy(HG.at[:, k % 2, k // 2], hg_out.at[:, k // 2, k % 2], out_sem.at[k]).wait()


def on_device(cotangent, expert_ids, route_weight, hidden, down_weight):
    nc = CHUNKS
    width = cotangent.shape[1]
    W = width // nc
    vmem = pltpu.VMEM
    dma = pltpu.SemaphoreType.DMA
    scratch = [
        vmem((8, 2, nc, 128, W), BF),
        vmem((8, 2, 8, 128), F32),
        vmem((8, 2, 64, 128), BF),
        vmem((8, 2, 2, 32, 128), BF),
        vmem((8, 2, 32, 128), BF),
        vmem((nc, 8, 2, 32, W), BF),
        vmem((nc, 8, 2, 2, 32, W), BF),
        vmem((8, 128, W), BF),
        vmem((8, 2, 2, 32, 1024), BF),
        vmem((8, 1024, 128), BF),
        vmem((nc, 16, 64, W), BF),
        vmem((4, 256, 1024), F32),
        vmem((nc, 4, 2, 128, W), BF),
        vmem((256, W), F32),
        vmem((256, W), F32),
        vmem((nc, 256, W), F32),
        vmem((nc, 2, 128, W), BF),
        vmem((nc, 2, 2, 128, W), BF),
        vmem((nc, 4, 64, W), BF),
        vmem((nc, 64, W), F32),
        vmem((nc, 3, 64, W), BF),
        vmem((nc, 64, W), BF),
        vmem((8, 2, 2, 32, 1024), BF),
        vmem((8, 8, 128), F32),
        vmem((8, 8, 128), F32),
        vmem((8, 128), F32),
        vmem((4, 8, 128), F32),
        vmem((128, 128), F32),
        dma((2 * nc + 4,)), dma((nc + 4,)),
        dma((8,)), dma((8,)),
        dma((nc,)), dma((nc,)),
        dma((nc, 2, 2, 4)), dma((nc, 2, 2, 4)),
        dma((nc + 1,)), dma((nc + 1,)),
        dma((3,)), dma((3,)),
        dma((4,)), dma((4,)),
        dma((nc, 2)), dma((nc, 2)),
        dma((nc, 2)), dma((nc, 2)),
        dma((nc, 3)), dma((nc, 3)),
        dma((7,)), dma((7,)),
        dma((3,)), dma((3,)),
    ]
    here = pl.BlockSpec(memory_space=pltpu.VMEM)
    anywhere = pl.BlockSpec(memory_space=pl.ANY)
    router_grad, hidden_grad, down_grad = pl.pallas_call(
        kernel,
        out_shape=(
            jax.ShapeDtypeStruct((128, 4), F32),
            jax.ShapeDtypeStruct((8, 2, 2, 32, 1024), BF),
            jax.ShapeDtypeStruct((64, width), BF),
        ),
        in_specs=[anywhere, here, here, anywhere, anywhere],
        out_specs=(here, anywhere, anywhere),
        scratch_shapes=scratch,
        compiler_params=pltpu.CompilerParams(collective_id=0, has_side_effects=True, vmem_limit_bytes=56 * 2**20),
        cost_estimate=pl.CostEstimate(flops=2 * 2 * 1024 * 1024 * 1536, bytes_accessed=6 * 2**20, transcendentals=0),
    )(cotangent, expert_ids, route_weight, hidden.reshape(8, 2, 2, 32, 1024), down_weight[0])
    return router_grad, hidden_grad.reshape(hidden.shape), down_grad[None]


def solution(mesh):
    in_specs = (
        P(("rep", "ep"), None),
        P(("rep", "ep"), None),
        P(("rep", "ep"), None),
        P("rep", "ep", None, None, None),
        P("ep", "rep", None),
    )
    out_specs = (P(("rep", "ep"), None), P("rep", "ep", None, None, None), P("ep", "rep", None))
    return jax.shard_map(on_device, mesh=mesh, in_specs=in_specs, out_specs=out_specs, check_vma=False)
```

time: 325 us -> 133 us (0.41)
  the two profiles are of different devices: /device:TPU:64 before, /device:TPU:1 now
where the time goes in v1:
time: 133 us; the launch traced here: 132 us
  Pallas kernels  123 us (92%)
  local copies, waits for them, and re-layouts  8.22 us (6%)
    pallas_call x1, Pallas kernels, on_device(): pl.pallas_call(kernel, out_shape=(jax.ShapeDtypeStruct((128, 4), F32), ja...  123 us
    unnamed x7, local copies, waits for them, and re-layouts  8.22 us

profile of v1, /device:TPU:1, one launch (start us, length us, event | category | flops | bytes accessed | tf_op | source)
XLA Modules:
  0.0 131.9 jit_solution(5707084907188538543)
XLA Ops:
  0.6 1.4 %copy.9.rw = bf16[128,4]{1,0:T(8,128)(2,1)} copy(bf16[128,4]{0,1:T(4,128)(2,1)} %param.7) | data formatting | bytes 2048 | tf_op args[2]
  2.0 1.4 %copy.8.ids = s32[128,4]{1,0:T(8,128)} copy(s32[128,4]{0,1:T(4,128)} %param.6) | data formatting | bytes 4096 | tf_op args[1]
  3.5 123.0 %shard_map.76 = (f32[128,4]{1,0:T(8,128)}, bf16[8,2,2,32,1024]{4,3,2,1,0:T(8,128)(2,1)}, bf16[64,1536]{1,0:T(8,128)(2,1)}) custom-call(bf16[128,1536]{1,0:T(8,128)(2,1)} %ct.1, s32[128,4]{1,0:T(8,128)} %copy.8.ids, bf16[128,4]{1,0:T(8,128)(2,1)} %copy.9.rw, bf16[8,2,2,32,1024]{4,3,2,1,0:T(8,128)(2,1)} %bitcast.6, bf16[64,1536]{1,0:T(8,128)(2,1)} %bitcast.7), custom_call_target="tpu_custom_call" | custom-call | flops 6442450944 | bytes 6291456 | tf_op jit(solution)/shard_map/pallas_call | solution.py:541
  126.5 1.5 %copy.10 = f32[128,4]{0,1:T(4,128)} copy(f32[128,4]{1,0:T(8,128)} %get-tuple-element.9) | data formatting | bytes 4096
  128.0 0.0 copy-start
  128.0 3.2 %copy.13 = bf16[1,1,32,32,1024]{4,3,2,1,0:T(8,128)(2,1)} copy(bf16[1,1,32,32,1024]{4,3,2,1,0:T(8,128)(2,1)} %bitcast.4) | data formatting | bytes 4194304
  131.2 0.0 copy-done
  131.2 0.7 copy.14
Async XLA Ops:
  128.0 3.2 %copy-start = (bf16[64,1536]{1,0:T(8,128)(2,1)S(1)}, bf16[64,1536]{1,0:T(8,128)(2,1)}, u32[]{:S(2)}) copy-start(bf16[64,1536]{1,0:T(8,128)(2,1)} %get-tuple-element.8) | copy-start | bytes 589828

commit v2 on v1

v2 whole, which is shorter than its diff:
```python
import functools

import jax
import jax.numpy as jnp
from jax import lax
from jax.experimental import pallas as pl
from jax.experimental.pallas import tpu as pltpu
from jax.sharding import PartitionSpec as P

MESH = pl.DeviceIdType.MESH
BF, F32 = jnp.bfloat16, jnp.float32
NT = (((1,), (1,)), ((), ()))
CHUNKS = 4


def remote(src, dst, send, recv, device):
    return pltpu.make_async_remote_copy(
        src_ref=src, dst_ref=dst, send_sem=send, recv_sem=recv, device_id=device, device_id_type=MESH
    )


def kernel(
    ct, ids, rw, hid_in, dw, rg, hg_out, dg_out,
    G, MT, PP, PF, SF, WR, WS, S, R, WB, hid, hidT, WG, back, PB, TA, TB, OWN, XH, XF, YB, YO, YR, DG, HG,
    SCB, L1, HT, MK,
    ld, out_sem, ms, mr, ys, yr, zs, zr, fs, fr, cs, cr, wys, wyr, wxs, wxr, xhs, xhr, xfs, xfr, yls, ylr,
    s1s, s1r,
):
    nc = G.shape[2]
    W = G.shape[4]
    rep, ep = lax.axis_index("rep"), lax.axis_index("ep")
    x, yl = rep // 4, rep % 4
    z, h, core = ep // 4, (ep // 2) % 2, ep % 2
    other = 1 - core
    ph = 1 - h

    def z_dev(k):
        return (rep, ((z + k + 8) % 8) * 4 + h * 2 + core)

    def column_dev(k, o):
        return (rep, ((z + k) % 8) * 4 + (h if o == 0 else ph) * 2 + core)

    def place(m):
        return (ph if m // 2 else h) * 2 + (other if m % 2 else core)

    def group_dev(k, m):
        return (rep, ((z + k) % 8) * 4 + place(m))

    def z_dev_other(k):
        return (rep, ((z + k + 8) % 8) * 4 + h * 2 + other)

    def x_dev(k):
        return (((x + k + 4) % 4) * 4 + yl, ep)

    def yl_dev(k):
        return (x * 4 + (yl + k) % 4, ep)

    def hc_dev(m):
        hh = ph if m // 2 else h
        cc = other if m % 2 else core
        return (rep, z * 4 + hh * 2 + cc)

    core_dev, y_dev = hc_dev(1), hc_dev(2)

    loads = []
    for c in range(nc):
        loads.append(pltpu.make_async_copy(ct.at[:, pl.ds(c * W, W)], G.at[z, h, c], ld.at[c]))
    w_loads = []
    for c in range(nc):
        w_loads.append(pltpu.make_async_copy(dw.at[:, pl.ds(c * W, W)], WG.at[c, rep], ld.at[nc + c]))
    h_loads = []
    for k in range(4):
        h_loads.append(pltpu.make_async_copy(hid_in.at[:, k // 2, k % 2], hid.at[:, k % 2, k // 2], ld.at[2 * nc + k]))
    for cp in loads + w_loads + h_loads:
        cp.start()

    peers = [group_dev(k, m) for k in range(8) for m in range(4) if (k, m) != (0, 0)]
    peers = peers + [x_dev(1), x_dev(-1)] + [yl_dev(k) for k in (1, 2, 3)]
    barrier = pltpu.get_barrier_semaphore()
    for p in peers:
        pl.semaphore_signal(barrier, inc=1, device_id=p, device_id_type=MESH)

    lane_e = lax.broadcasted_iota(jnp.int32, (128, 128), 1).astype(F32)
    sub_t = lax.broadcasted_iota(jnp.int32, (128, 128), 0).astype(F32)
    ids_row, weight_row = ids[...].astype(F32), rw[...].astype(F32)
    rows = jnp.zeros((128, 128), F32)
    for k in range(4):
        rows = jnp.where(sub_t == k, ids_row[k : k + 1], rows)
        rows = jnp.where(sub_t == 4 + k, weight_row[k : k + 1], rows)
    columns = rows.T
    idf, wf = columns[:, 0:4], columns[:, 4:8]
    named = jnp.zeros((128, 128), F32)
    for k in range(4):
        named = named + jnp.where(idf[:, k : k + 1] == lane_e, 1.0, 0.0)
    before = jnp.where(sub_t > lane_e, 1.0, 0.0)
    count = jnp.dot(before.astype(BF), named.astype(BF), preferred_element_type=F32)
    packed = jnp.zeros((128, 128), F32)
    for k in range(4):
        own = idf[:, k : k + 1]
        rank = jnp.sum(jnp.where(own == lane_e, count, 0.0), axis=1, keepdims=True)
        packed = jnp.where(lane_e == k, own * 32.0 + rank, packed)
        packed = jnp.where(lane_e == 4 + k, wf[:, k : k + 1], packed)
        packed = jnp.where(lane_e == 8 + k, rank, packed)
        packed = jnp.where(lane_e == 12 + k, own, packed)
    turned = packed.T
    MT[z, h] = turned[0:8]
    spot = lax.broadcasted_iota(jnp.int32, (256, 128), 0)
    expert_of = jnp.where(spot % 8 == 0, (spot // 32) * 4 + (spot // 8) % 4, -1).astype(F32)
    for k in range(4):
        HT[:, k * 128 : k * 128 + 128] = jnp.where(turned[12 + k : 13 + k] == expert_of, 1.0, 0.0)
        slot = turned[8 + k : 9 + k] + ((core * 2 + h) * 32).astype(F32)
        MK[:, k * 128 : k * 128 + 128] = jnp.where(slot == sub_t, 1.0, 0.0)

    pl.semaphore_wait(barrier, len(peers))

    others = [(k, o) for k in range(8) for o in (0, 1) if (k, o) != (0, 0)]

    def meta(k, o):
        return remote(MT.at[z, h], MT.at[z, h], ms.at[k, o], mr.at[k, o], column_dev(k, o))

    def meta_in(k, o):
        blk = MT.at[(z - k + 8) % 8, h if o == 0 else ph]
        return remote(blk, blk, ms.at[k, o], mr.at[k, o], column_dev(8 - k, o))

    def tok_y(c):
        return remote(G.at[z, h, c], G.at[z, h, c], ys.at[c], yr.at[c], y_dev)

    def tok_y_in(c):
        return remote(G.at[z, ph, c], G.at[z, ph, c], ys.at[c], yr.at[c], y_dev)

    def far(way, d):
        return (z - d + 8) % 8 if way == 0 else (z + d) % 8

    def hi(which):
        return h if which == 0 else ph

    def tok_z(c, which, way, s):
        blk = G.at[far(way, s), hi(which), c]
        return remote(blk, blk, zs.at[c, which, way, s], zr.at[c, which, way, s], z_dev(1 if way == 0 else -1))

    def tok_z_in(c, which, way, s):
        blk = G.at[far(way, s + 1), hi(which), c]
        return remote(blk, blk, zs.at[c, which, way, s], zr.at[c, which, way, s], z_dev(-1 if way == 0 else 1))

    def tok_far(c, way, to):
        k = 1 if way == 0 else -1
        device = z_dev(k) if to == 0 else z_dev_other(k)
        return remote(SF.at[c, way, to], R.at[c, 7, core, hi(way)], fs.at[c, way, to], fr.at[c, way, to], device)

    def tok_far_in(c, way, to):
        k = -1 if way == 0 else 1
        device = z_dev(k) if to == 0 else z_dev_other(k)
        return remote(SF.at[c, way, to], R.at[c, 7, core if to == 0 else other, hi(way)], fs.at[c, way, to], fr.at[c, way, to], device)

    def swap(c):
        return remote(S.at[c], R.at[c, pl.ds(0, 7), core], cs.at[c], cr.at[c], core_dev)

    def swap_in(c):
        return remote(S.at[c], R.at[c, pl.ds(0, 7), other], cs.at[c], cr.at[c], core_dev)

    def plane(n):
        return (z + n + 5) % 8

    def swap_w():
        return remote(WS, WR.at[:, core], cs.at[nc], cr.at[nc], core_dev)

    def swap_w_in():
        return remote(WS, WR.at[:, other], cs.at[nc], cr.at[nc], core_dev)

    def w_y(k):
        blk = WG.at[:, rep]
        return remote(blk, blk, wys.at[k - 1], wyr.at[k - 1], yl_dev(k))

    def w_y_in(k):
        blk = WG.at[:, x * 4 + (yl - k + 4) % 4]
        return remote(blk, blk, wys.at[k - 1], wyr.at[k - 1], yl_dev(4 - k))

    def w_x(k, way):
        blk = WG.at[:, x * 4 + (yl + k) % 4]
        return remote(blk, blk, wxs.at[k, way], wxr.at[k, way], x_dev(1 if way == 0 else -1))

    def w_x_in(k, way):
        o = (x - 1 + 4) % 4 if way == 0 else (x + 1) % 4
        blk = WG.at[:, o * 4 + (yl + k) % 4]
        return remote(blk, blk, wxs.at[k, way], wxr.at[k, way], x_dev(-1 if way == 0 else 1))

    def w_half(k, way):
        o = (x - 1 + 4) % 4 if way == 0 else (x + 1) % 4
        blk = WG.at[:, o * 4 + (yl + k) % 4, pl.ds(32 * way, 32)]
        return remote(blk, blk, wxs.at[k, 2 + way], wxr.at[k, 2 + way], x_dev(1 if way == 0 else -1))

    def w_half_in(k, way):
        o = (x + 2) % 4
        blk = WG.at[:, o * 4 + (yl + k) % 4, pl.ds(32 * way, 32)]
        return remote(blk, blk, wxs.at[k, 2 + way], wxr.at[k, 2 + way], x_dev(-1 if way == 0 else 1))

    x_two, x_up, x_down = (x + 2) % 4, (x + 1) % 4, (x + 3) % 4

    def x_half(c, side):
        return remote(PB.at[c, x_two, side], XH.at[c, side], xhs.at[c, side], xhr.at[c, side], x_dev(-1 if side == 0 else 1))

    def x_full(c, side):
        return remote(PB.at[c, x_down if side == 0 else x_up], XF.at[c, side], xfs.at[c, side], xfr.at[c, side], x_dev(-1 if side == 0 else 1))

    def y_part(c, k):
        return remote(YB.at[c, (yl + k) % 4], YR.at[c, k - 1], yls.at[c, k - 1], ylr.at[c, k - 1], yl_dev(k))

    def score(k, m):
        return remote(SCB.at[(z + k) % 8], L1.at[z, h * 2 + core], s1s.at[k, m], s1r.at[k, m], group_dev(k, m))

    def score_in(k, m):
        o = (z - k + 8) % 8
        return remote(SCB.at[o], L1.at[o, place(m)], s1s.at[k, m], s1r.at[k, m], group_dev(8 - k, m))

    everyone = [(k, m) for k in range(8) for m in range(4) if (k, m) != (0, 0)]

    for k, o in others:
        meta(k, o).start()
    for c in range(nc):
        loads[c].wait()
        if c == 0:
            tok_y(c).start()
        if c < 3:
            for way in (0, 1):
                tok_z(c, 0, way, 0).start()
    for c in range(nc):
        w_loads[c].wait()
    for k in (1, 2, 3):
        w_y(k).start()
    for way in (0, 1):
        w_x(0, way).start()

    def turn(q, _):
        blk = hid[q].reshape(128, 1024)
        hidT[q] = blk.T
        return 0


    def clear(q, _):
        back[q] = jnp.zeros((256, 1024), F32)
        return 0


    row = lax.broadcasted_iota(jnp.int32, (64, 128), 0).astype(F32)

    def match(m, first, second):
        target = jnp.where(row < 32.0, row + first.astype(F32), row - 32.0 + second.astype(F32))
        pick = jnp.zeros((64, 128), F32)
        weight = jnp.zeros((64, 128), F32)
        for k in range(4):
            same = m[k : k + 1, :] == target
            pick = jnp.where(same, 1.0, pick)
            weight = jnp.where(same, m[4 + k : 5 + k, :], weight)
        return pick.astype(BF), weight.astype(BF)

    def select(n, _):
        zz, hh = n // 2, n % 2
        base = (z * 4 + h * 2) * 32
        pick, weight = match(MT[zz, hh], base + core * 32, base + other * 32)
        PP[zz, hh] = pick
        wide = jnp.dot(weight, jnp.ones((128, 128), BF), preferred_element_type=F32).astype(BF)
        WR[zz, core, hh] = wide[0:32]
        WS[zz, hh] = wide[32:64]
        return 0

    def select_far():
        for way in (0, 1):
            base = (((z + 1) % 8 if way == 0 else (z + 7) % 8) * 4 + h * 2) * 32
            PF[way] = match(MT[far(way, 3), hi(way)], base + core * 32, base + other * 32)[0]

    def pack(c, zz, hh, n):
        rows = jnp.dot(PP[zz, hh], G[zz, hh, c], preferred_element_type=F32).astype(BF)
        R[c, n, core, hh] = rows[0:32]
        S[c, n, hh] = rows[32:64]

    def forward(c, s, both=(0, 1)):
        for which in both:
            for way in (0, 1):
                tok_z_in(c, which, way, s - 1).wait_recv()
                if s < 3:
                    tok_z(c, which, way, s).start()
                elif which == way:
                    rows = jnp.dot(PF[way], G[far(way, 3), hi(way), c], preferred_element_type=F32).astype(BF)
                    SF[c, way, 0] = rows[0:32]
                    SF[c, way, 1] = rows[32:64]
                    tok_far(c, way, 0).start()
                    tok_far(c, way, 1).start()

    def pack_far(c, d):
        for which in (0, 1):
            for way in (0, 1):
                pack(c, far(way, d), hi(which), 3 - d if way == 0 else 3 + d)

    def partial(q):
        total = jnp.zeros((256, W), F32)
        for n in range(8):
            total = total + jnp.dot(hidT[plane(n), pl.ds(q * 256, 256)], WB[n], preferred_element_type=F32)
        return total

    def backward(c):
        def rows(q, _):
            r = R[c, pl.ds(q * 2, 2)].reshape(256, W)
            w = WG[c].reshape(1024, W)
            back[q] = back[q] + lax.dot_general(r, w, NT, preferred_element_type=F32)
            return 0

        lax.fori_loop(0, 4, rows, 0)

    def weigh(c):
        def block(n, _):
            wide = WR[plane(n)].reshape(128, 128).astype(F32)
            wide = jnp.concatenate([wide] * (W // 128), axis=1)
            WB[n] = (R[c, n].reshape(128, W).astype(F32) * wide).astype(BF)
            return 0

        lax.fori_loop(0, 8, block, 0)

    def clean(c):
        tok_y(c).wait_send()
        for way in (0, 1):
            for s in range(3):
                tok_z(c, 0, way, s).wait_send()
                tok_z(c, 1, way, s).wait_send()
            for to in (0, 1):
                tok_far(c, way, to).wait_send()
        swap(c).wait_send()
        for side in (0, 1):
            x_half(c, side).wait_send()

    def reduce_y(d):
        x_full(d, 0).wait_recv()
        x_full(d, 1).wait_recv()
        got = XF[d, 0].reshape(256, W).astype(F32) + XF[d, 1].reshape(256, W).astype(F32)
        OWN[d] = OWN[d] + got
        YB[d] = OWN[d].reshape(4, 64, W).astype(BF)
        YO[d] = OWN[d, pl.ds(yl * 64, 64)]
        for k in (1, 2, 3):
            y_part(d, k).start()
        clean(d)

    def turn_of(i, _):
        c, e = i - 4, i - 5
        at = [(i >= s) & (i - s < nc) for s in range(7)]

        @pl.when(i == 0)
        def _():
            forward(0, 1, (0,))

        for s in (3, 2, 1):

            @pl.when((i >= s - 2) & (i - s + 2 < nc))
            def _():
                forward(i - s + 2, s, (0,))

        @pl.when(i + 3 < nc)
        def _():
            for way in (0, 1):
                tok_z(i + 3, 0, way, 0).start()

        for s in (3, 2, 1):

            @pl.when(at[s])
            def _():
                forward(i - s, s, (1,))

        @pl.when(i == nc // 2)
        def _():
            for k in (1, 2, 3):
                w_y_in(k).wait_recv()
                for way in (0, 1):
                    w_x(4 - k, way).start()

        @pl.when(at[0])
        def _():
            tok_y_in(i).wait_recv()
            for way in (0, 1):
                tok_z(i, 1, way, 0).start()

        @pl.when(i + 1 < nc)
        def _():
            tok_y(i + 1).start()

        @pl.when(i == 0)
        def _():
            for k, o in others:
                meta_in(k, o).wait_recv()
            select_far()
            lax.fori_loop(0, 16, select, 0)
            swap_w().start()

        @pl.when(at[4])
        def _():
            swap_in(c).wait_recv()
            for way in (0, 1):
                for to in (0, 1):
                    tok_far_in(c, way, to).wait_recv()
            weigh(c)
            PB[c, x_two] = partial(x_two).astype(BF).reshape(2, 128, W)
            x_half(c, 0).start()
            x_half(c, 1).start()
            TA[c % 2] = partial(x_down)
            TB[c % 2] = partial(x_up)
            OWN[c] = partial(x)

        @pl.when((i >= 7) & (i <= nc + 3))
        def _():
            reduce_y(i - 7)

        for s in (3, 2, 1):

            @pl.when(at[s])
            def _():
                pack_far(i - s, s)

        @pl.when(at[3])
        def _():
            swap(i - 3).start()

        @pl.when(at[0])
        def _():
            pack(i, z, h, 3)
            pack(i, z, ph, 3)

        @pl.when(i == 0)
        def _():
            for k in range(4):
                h_loads[k].wait()
            lax.fori_loop(0, 8, turn, 0)
            lax.fori_loop(0, 4, clear, 0)
            swap_w_in().wait_recv()

        @pl.when(i == 0)
        def _():
            for way in (0, 1):
                w_x_in(0, way).wait_recv()
                w_half(0, way).start()

        @pl.when(i == nc // 2 + 1)
        def _():
            for k in (1, 2, 3):
                for way in (0, 1):
                    w_x_in(k, way).wait_recv()
                    w_half(k, way).start()

        @pl.when(at[5])
        def _():
            x_half(e, 0).wait_recv()
            PB[e, x_down, 0] = (TA[e % 2, 0:128] + XH[e, 0].astype(F32)).astype(BF)
            PB[e, x_down, 1] = TA[e % 2, 128:256].astype(BF)
            x_full(e, 0).start()
            x_half(e, 1).wait_recv()
            PB[e, x_up, 0] = TB[e % 2, 0:128].astype(BF)
            PB[e, x_up, 1] = (TB[e % 2, 128:256] + XH[e, 1].astype(F32)).astype(BF)
            x_full(e, 1).start()

        @pl.when(i == nc + 3)
        def _():
            for k in range(4):
                for way in (0, 1):
                    w_half_in(k, way).wait_recv()
            lax.fori_loop(0, nc // 2, lambda n, _: (backward(n), 0)[1], 0)
            reduce_y(nc - 3)

        @pl.when(i == nc + 4)
        def _():
            lax.fori_loop(nc // 2, nc, lambda n, _: (backward(n), 0)[1], 0)
            reduce_y(nc - 2)

            def finish(q, _):
                def half(u, _):
                    t = back[q, pl.ds(u * 128, 128)]
                    n = plane(q * 2 + u)
                    wide = WR[n].reshape(128, 128).astype(F32)
                    wide = jnp.concatenate([wide] * 8, axis=1)
                    HG[n] = (wide * t).astype(BF).reshape(2, 2, 32, 1024)
                    col = jnp.sum(hid[n].reshape(128, 1024).astype(F32) * t, axis=1, keepdims=True)
                    SCB[n] = jnp.broadcast_to(col, (128, 128)).T[0:8, :]
                    return 0

                lax.fori_loop(0, 2, half, 0)
                return 0

            lax.fori_loop(0, 4, finish, 0)
            for k in range(4):
                pltpu.make_async_copy(HG.at[:, k % 2, k // 2], hg_out.at[:, k // 2, k % 2], out_sem.at[k]).start()
            for k, m in everyone:
                score(k, m).start()
            L1[z, h * 2 + core] = SCB[z]

        return 0

    lax.fori_loop(0, nc + 5, turn_of, 0)
    reduce_y(nc - 1)

    def total_of(f, _):
        total = YO[f]
        for k in (1, 2, 3):
            y_part(f, k).wait_recv()
            total = total + YR[f, k - 1].astype(F32)
        DG[f] = total.astype(BF)
        pltpu.make_async_copy(DG.at[f], dg_out.at[:, pl.ds(pl.multiple_of(f * W, 128), W)], out_sem.at[4 + f]).start()
        return 0

    lax.fori_loop(0, nc, total_of, 0)

    for k, m in everyone:
        score_in(k, m).wait_recv()
    value = L1[...].reshape(256, 128)
    rows = lax.dot_general(value, HT[...], (((0,), (0,)), ((), ())), preferred_element_type=F32, precision=lax.Precision.HIGHEST)
    picked = jnp.sum(rows * MK[...], axis=0, keepdims=True)
    for k in range(4):
        rg[k : k + 1, :] = picked[:, k * 128 : k * 128 + 128]

    for k, o in others:
        meta(k, o).wait_send()
    for k, m in everyone:
        score(k, m).wait_send()
    for k in (1, 2, 3):
        w_y(k).wait_send()
    for k in range(4):
        for way in (0, 1):
            w_x(k, way).wait_send()
            w_half(k, way).wait_send()
    swap_w().wait_send()

    def drain(c, _):
        for side in (0, 1):
            x_full(c, side).wait_send()
        for k in (1, 2, 3):
            y_part(c, k).wait_send()
        pltpu.make_async_copy(DG.at[c], dg_out.at[:, pl.ds(pl.multiple_of(c * W, 128), W)], out_sem.at[4 + c]).wait()
        return 0

    lax.fori_loop(0, nc, drain, 0)
    for k in range(4):
        pltpu.make_async_copy(HG.at[:, k % 2, k // 2], hg_out.at[:, k // 2, k % 2], out_sem.at[k]).wait()


def on_device(cotangent, expert_ids, route_weight, hidden, down_weight):
    nc = CHUNKS
    width = cotangent.shape[1]
    W = width // nc
    vmem = pltpu.VMEM
    dma = pltpu.SemaphoreType.DMA
    scratch = [
        vmem((8, 2, nc, 128, W), BF),
        vmem((8, 2, 8, 128), F32),
        vmem((8, 2, 64, 128), BF),
        vmem((2, 64, 128), BF),
        vmem((nc, 2, 2, 32, W), BF),
        vmem((8, 2, 2, 32, 128), BF),
        vmem((8, 2, 32, 128), BF),
        vmem((nc, 7, 2, 32, W), BF),
        vmem((nc, 8, 2, 2, 32, W), BF),
        vmem((8, 128, W), BF),
        vmem((8, 2, 2, 32, 1024), BF),
        vmem((8, 1024, 128), BF),
        vmem((nc, 16, 64, W), BF),
        vmem((4, 256, 1024), F32),
        vmem((nc, 4, 2, 128, W), BF),
        vmem((2, 256, W), F32),
        vmem((2, 256, W), F32),
        vmem((nc, 256, W), F32),
        vmem((nc, 2, 128, W), BF),
        vmem((nc, 2, 2, 128, W), BF),
        vmem((nc, 4, 64, W), BF),
        vmem((nc, 64, W), F32),
        vmem((nc, 3, 64, W), BF),
        vmem((nc, 64, W), BF),
        vmem((8, 2, 2, 32, 1024), BF),
        vmem((8, 8, 128), F32),
        vmem((8, 4, 8, 128), F32),
        vmem((256, 512), F32),
        vmem((128, 512), F32),
        dma((2 * nc + 4,)), dma((nc + 4,)),
        dma((8, 2)), dma((8, 2)),
        dma((nc,)), dma((nc,)),
        dma((nc, 2, 2, 3)), dma((nc, 2, 2, 3)),
        dma((nc, 2, 2)), dma((nc, 2, 2)),
        dma((nc + 1,)), dma((nc + 1,)),
        dma((3,)), dma((3,)),
        dma((4, 4)), dma((4, 4)),
        dma((nc, 2)), dma((nc, 2)),
        dma((nc, 2)), dma((nc, 2)),
        dma((nc, 3)), dma((nc, 3)),
        dma((8, 4)), dma((8, 4)),
    ]
    here = pl.BlockSpec(memory_space=pltpu.VMEM)
    anywhere = pl.BlockSpec(memory_space=pl.ANY)
    router_grad, hidden_grad, down_grad = pl.pallas_call(
        kernel,
        out_shape=(
            jax.ShapeDtypeStruct((4, 128), F32),
            jax.ShapeDtypeStruct((8, 2, 2, 32, 1024), BF),
            jax.ShapeDtypeStruct((64, width), BF),
        ),
        in_specs=[anywhere, here, here, anywhere, anywhere],
        out_specs=(here, anywhere, anywhere),
        scratch_shapes=scratch,
        compiler_params=pltpu.CompilerParams(collective_id=0, has_side_effects=True, vmem_limit_bytes=56 * 2**20),
        cost_estimate=pl.CostEstimate(flops=2 * 2 * 1024 * 1024 * 1536, bytes_accessed=6 * 2**20, transcendentals=0),
    )(cotangent, expert_ids.T, route_weight.T, hidden.reshape(8, 2, 2, 32, 1024), down_weight[0])
    return router_grad.T, hidden_grad.reshape(hidden.shape), down_grad[None]


def solution(mesh):
    in_specs = (
        P(("rep", "ep"), None),
        P(("rep", "ep"), None),
        P(("rep", "ep"), None),
        P("rep", "ep", None, None, None),
        P("ep", "rep", None),
    )
    out_specs = (P(("rep", "ep"), None), P("rep", "ep", None, None, None), P("ep", "rep", None))
    return jax.shard_map(on_device, mesh=mesh, in_specs=in_specs, out_specs=out_specs, check_vma=False)
```

time: 133 us -> 122 us (0.917)
  Pallas kernels: 123 us -> 116 us
  local copies, waits for them, and re-layouts: 8.22 us -> 5.16 us
    pallas_call x1, Pallas kernels: 123 us -> 116 us  [on_device(): pl.pallas_call(kernel, out_shape=(jax.ShapeDtypeStruct((4, 128), F32), ja...]
    unnamed x7 -> x5, local copies, waits for them, and re-layouts: 8.22 us -> 5.16 us
where the time goes in v2:
time: 122 us
  Pallas kernels  116 us (95%)
  local copies, waits for them, and re-layouts  5.16 us (4%)
    pallas_call x1, Pallas kernels, on_device(): pl.pallas_call(kernel, out_shape=(jax.ShapeDtypeStruct((4, 128), F32), ja...  116 us
    unnamed x5, local copies, waits for them, and re-layouts  5.16 us

profile of v2, /device:TPU:1, one launch (start us, length us, event | category | flops | bytes accessed | tf_op | source)
XLA Modules:
  0.0 121.8 jit_solution(16031561290986130975)
XLA Ops:
  0.6 116.0 %shard_map.76 = (f32[4,128]{1,0:T(4,128)}, bf16[8,2,2,32,1024]{4,3,2,1,0:T(8,128)(2,1)}, bf16[64,1536]{1,0:T(8,128)(2,1)}) custom-call(bf16[128,1536]{1,0:T(8,128)(2,1)} %ct.1, s32[4,128]{1,0:T(4,128)} %bitcast.12, bf16[4,128]{1,0:T(4,128)(2,1)} %bitcast.13, bf16[8,2,2,32,1024]{4,3,2,1,0:T(8,128)(2,1)} %bitcast.10, bf16[64,1536]{1,0:T(8,128)(2,1)} %bitcast.11), custom_call_target="tpu_custom_call" | custom-call | flops 6442450944 | bytes 6291456 | tf_op jit(solution)/shard_map/pallas_call | solution.py:590
  116.6 1.3 %copy.11 = f32[128,4]{0,1:T(4,128)} copy(f32[128,4]{0,1:T(4,128)} %bitcast.9) | data formatting | bytes 4096
  117.9 0.0 copy-start
  117.9 3.2 %copy.12 = bf16[1,1,32,32,1024]{4,3,2,1,0:T(8,128)(2,1)} copy(bf16[1,1,32,32,1024]{4,3,2,1,0:T(8,128)(2,1)} %bitcast.7) | data formatting | bytes 4194304
  121.1 0.0 copy-done
  121.1 0.7 copy.13
Async XLA Ops:
  117.9 3.2 %copy-start = (bf16[64,1536]{1,0:T(8,128)(2,1)S(1)}, bf16[64,1536]{1,0:T(8,128)(2,1)}, u32[]{:S(2)}) copy-start(bf16[64,1536]{1,0:T(8,128)(2,1)} %get-tuple-element.8) | copy-start | bytes 589828

commit v3 on v2

--- a/solution.py
+++ b/solution.py
@@ -10,7 +10,7 @@
 MESH = pl.DeviceIdType.MESH
 BF, F32 = jnp.bfloat16, jnp.float32
 NT = (((1,), (1,)), ((), ()))
-CHUNKS = 4
+CHUNKS = 6
 
 
 def remote(src, dst, send, recv, device):
@@ -225,8 +225,6 @@
                 tok_z(c, 0, way, 0).start()
     for c in range(nc):
         w_loads[c].wait()
-    for k in (1, 2, 3):
-        w_y(k).start()
     for way in (0, 1):
         w_x(0, way).start()
 
@@ -327,6 +325,16 @@
         for side in (0, 1):
             x_half(c, side).wait_send()
 
+    def send_full(e):
+        x_half(e, 0).wait_recv()
+        PB[e, x_down, 0] = (TA[e % 3, 0:128] + XH[e, 0].astype(F32)).astype(BF)
+        PB[e, x_down, 1] = TA[e % 3, 128:256].astype(BF)
+        x_full(e, 0).start()
+        x_half(e, 1).wait_recv()
+        PB[e, x_up, 0] = TB[e % 3, 0:128].astype(BF)
+        PB[e, x_up, 1] = (TB[e % 3, 128:256] + XH[e, 1].astype(F32)).astype(BF)
+        x_full(e, 1).start()
+
     def reduce_y(d):
         x_full(d, 0).wait_recv()
         x_full(d, 1).wait_recv()
@@ -339,12 +347,18 @@
         clean(d)
 
     def turn_of(i, _):
-        c, e = i - 4, i - 5
+        c = i - 4
         at = [(i >= s) & (i - s < nc) for s in range(7)]
 
         @pl.when(i == 0)
         def _():
             forward(0, 1, (0,))
+            tok_y(1).start()
+            w_y(1).start()
+
+        @pl.when(i == 1)
+        def _():
+            w_y(3).start()
 
         for s in (3, 2, 1):
 
@@ -370,18 +384,26 @@
                 for way in (0, 1):
                     w_x(4 - k, way).start()
 
+        @pl.when(i == nc // 2 + 2)
+        def _():
+            for k in (1, 2, 3):
+                for way in (0, 1):
+                    w_x_in(k, way).wait_recv()
+                    w_half(k, way).start()
+
         @pl.when(at[0])
         def _():
             tok_y_in(i).wait_recv()
             for way in (0, 1):
                 tok_z(i, 1, way, 0).start()
 
-        @pl.when(i + 1 < nc)
-        def _():
-            tok_y(i + 1).start()
+        @pl.when(i + 2 < nc)
+        def _():
+            tok_y(i + 2).start()
 
         @pl.when(i == 0)
         def _():
+            w_y(2).start()
             for k, o in others:
                 meta_in(k, o).wait_recv()
             select_far()
@@ -398,13 +420,20 @@
             PB[c, x_two] = partial(x_two).astype(BF).reshape(2, 128, W)
             x_half(c, 0).start()
             x_half(c, 1).start()
-            TA[c % 2] = partial(x_down)
-            TB[c % 2] = partial(x_up)
+
+        @pl.when((i >= 6) & (i <= nc + 3))
+        def _():
+            send_full(i - 6)
+
+        @pl.when(at[4])
+        def _():
+            TA[c % 3] = partial(x_down)
+            TB[c % 3] = partial(x_up)
             OWN[c] = partial(x)
 
-        @pl.when((i >= 7) & (i <= nc + 3))
-        def _():
-            reduce_y(i - 7)
+        @pl.when((i >= 8) & (i <= nc + 3))
+        def _():
+            reduce_y(i - 8)
 
         for s in (3, 2, 1):
 
@@ -435,36 +464,22 @@
                 w_x_in(0, way).wait_recv()
                 w_half(0, way).start()
 
-        @pl.when(i == nc // 2 + 1)
-        def _():
-            for k in (1, 2, 3):
-                for way in (0, 1):
-                    w_x_in(k, way).wait_recv()
-                    w_half(k, way).start()
-
-        @pl.when(at[5])
-        def _():
-            x_half(e, 0).wait_recv()
-            PB[e, x_down, 0] = (TA[e % 2, 0:128] + XH[e, 0].astype(F32)).astype(BF)
-            PB[e, x_down, 1] = TA[e % 2, 128:256].astype(BF)
-            x_full(e, 0).start()
-            x_half(e, 1).wait_recv()
-            PB[e, x_up, 0] = TB[e % 2, 0:128].astype(BF)
-            PB[e, x_up, 1] = (TB[e % 2, 128:256] + XH[e, 1].astype(F32)).astype(BF)
-            x_full(e, 1).start()
-
         @pl.when(i == nc + 3)
         def _():
+            send_full(nc - 2)
             for k in range(4):
                 for way in (0, 1):
                     w_half_in(k, way).wait_recv()
             lax.fori_loop(0, nc // 2, lambda n, _: (backward(n), 0)[1], 0)
+            reduce_y(nc - 4)
+
+        @pl.when(i == nc + 4)
+        def _():
+            send_full(nc - 1)
             reduce_y(nc - 3)
-
-        @pl.when(i == nc + 4)
-        def _():
-            lax.fori_loop(nc // 2, nc, lambda n, _: (backward(n), 0)[1], 0)
+            lax.fori_loop(nc // 2, nc - 1, lambda n, _: (backward(n), 0)[1], 0)
             reduce_y(nc - 2)
+            backward(nc - 1)
 
             def finish(q, _):
                 def half(u, _):
@@ -558,8 +573,8 @@
         vmem((nc, 16, 64, W), BF),
         vmem((4, 256, 1024), F32),
         vmem((nc, 4, 2, 128, W), BF),
-        vmem((2, 256, W), F32),
-        vmem((2, 256, W), F32),
+        vmem((3, 256, W), F32),
+        vmem((3, 256, W), F32),
         vmem((nc, 256, W), F32),
         vmem((nc, 2, 128, W), BF),
         vmem((nc, 2, 2, 128, W), BF),

time: 122 us -> 118 us (0.967)
  Pallas kernels: 116 us -> 112 us
    pallas_call x1, Pallas kernels: 116 us -> 112 us  [on_device(): pl.pallas_call(kernel, out_shape=(jax.ShapeDtypeStruct((4, 128), F32), ja...]
where the time goes in v3:
time: 118 us
  Pallas kernels  112 us (95%)
  local copies, waits for them, and re-layouts  5.16 us (4%)
    pallas_call x1, Pallas kernels, on_device(): pl.pallas_call(kernel, out_shape=(jax.ShapeDtypeStruct((4, 128), F32), ja...  112 us
    unnamed x5, local copies, waits for them, and re-layouts  5.16 us

profile of v3, /device:TPU:1, one launch (start us, length us, event | category | flops | bytes accessed | tf_op | source)
XLA Modules:
  0.0 117.8 jit_solution(7097554353958922924)
XLA Ops:
  0.6 112.0 %shard_map.76 = (f32[4,128]{1,0:T(4,128)}, bf16[8,2,2,32,1024]{4,3,2,1,0:T(8,128)(2,1)}, bf16[64,1536]{1,0:T(8,128)(2,1)}) custom-call(bf16[128,1536]{1,0:T(8,128)(2,1)} %ct.1, s32[4,128]{1,0:T(4,128)} %bitcast.12, bf16[4,128]{1,0:T(4,128)(2,1)} %bitcast.13, bf16[8,2,2,32,1024]{4,3,2,1,0:T(8,128)(2,1)} %bitcast.10, bf16[64,1536]{1,0:T(8,128)(2,1)} %bitcast.11), custom_call_target="tpu_custom_call" | custom-call | flops 6442450944 | bytes 6291456 | tf_op jit(solution)/shard_map/pallas_call | solution.py:605
  112.7 1.3 %copy.11 = f32[128,4]{0,1:T(4,128)} copy(f32[128,4]{0,1:T(4,128)} %bitcast.9) | data formatting | bytes 4096
  113.9 0.0 copy-start
  113.9 3.2 %copy.12 = bf16[1,1,32,32,1024]{4,3,2,1,0:T(8,128)(2,1)} copy(bf16[1,1,32,32,1024]{4,3,2,1,0:T(8,128)(2,1)} %bitcast.7) | data formatting | bytes 4194304
  117.1 0.0 copy-done
  117.1 0.7 copy.13
Async XLA Ops:
  113.9 3.2 %copy-start = (bf16[64,1536]{1,0:T(8,128)(2,1)S(1)}, bf16[64,1536]{1,0:T(8,128)(2,1)}, u32[]{:S(2)}) copy-start(bf16[64,1536]{1,0:T(8,128)(2,1)} %get-tuple-element.8) | copy-start | bytes 589828

commit v4 on v3

--- a/solution.py
+++ b/solution.py
@@ -464,13 +464,17 @@
                 w_x_in(0, way).wait_recv()
                 w_half(0, way).start()
 
-        @pl.when(i == nc + 3)
-        def _():
-            send_full(nc - 2)
+        @pl.when(i == nc + 2)
+        def _():
             for k in range(4):
                 for way in (0, 1):
                     w_half_in(k, way).wait_recv()
-            lax.fori_loop(0, nc // 2, lambda n, _: (backward(n), 0)[1], 0)
+            backward(0)
+
+        @pl.when(i == nc + 3)
+        def _():
+            send_full(nc - 2)
+            lax.fori_loop(1, nc // 2, lambda n, _: (backward(n), 0)[1], 0)
             reduce_y(nc - 4)
 
         @pl.when(i == nc + 4)

time: 118 us -> 118 us (level)
  no operation moved by 1% of the time
where the time goes in v4:
time: 118 us
  Pallas kernels  112 us (95%)
  local copies, waits for them, and re-layouts  5.16 us (4%)
    pallas_call x1, Pallas kernels, on_device(): pl.pallas_call(kernel, out_shape=(jax.ShapeDtypeStruct((4, 128), F32), ja...  112 us
    unnamed x5, local copies, waits for them, and re-layouts  5.16 us

profile of v4, /device:TPU:1, one launch (start us, length us, event | category | flops | bytes accessed | tf_op | source)
XLA Modules:
  0.0 118.0 jit_solution(3899205602570738236)
XLA Ops:
  0.6 112.2 %shard_map.76 = (f32[4,128]{1,0:T(4,128)}, bf16[8,2,2,32,1024]{4,3,2,1,0:T(8,128)(2,1)}, bf16[64,1536]{1,0:T(8,128)(2,1)}) custom-call(bf16[128,1536]{1,0:T(8,128)(2,1)} %ct.1, s32[4,128]{1,0:T(4,128)} %bitcast.12, bf16[4,128]{1,0:T(4,128)(2,1)} %bitcast.13, bf16[8,2,2,32,1024]{4,3,2,1,0:T(8,128)(2,1)} %bitcast.10, bf16[64,1536]{1,0:T(8,128)(2,1)} %bitcast.11), custom_call_target="tpu_custom_call" | custom-call | flops 6442450944 | bytes 6291456 | tf_op jit(solution)/shard_map/pallas_call | solution.py:609
  112.9 1.3 %copy.11 = f32[128,4]{0,1:T(4,128)} copy(f32[128,4]{0,1:T(4,128)} %bitcast.9) | data formatting | bytes 4096
  114.1 0.0 copy-start
  114.1 3.2 %copy.12 = bf16[1,1,32,32,1024]{4,3,2,1,0:T(8,128)(2,1)} copy(bf16[1,1,32,32,1024]{4,3,2,1,0:T(8,128)(2,1)} %bitcast.7) | data formatting | bytes 4194304
  117.4 0.0 copy-done
  117.4 0.7 copy.13
Async XLA Ops:
  114.1 3.2 %copy-start = (bf16[64,1536]{1,0:T(8,128)(2,1)S(1)}, bf16[64,1536]{1,0:T(8,128)(2,1)}, u32[]{:S(2)}) copy-start(bf16[64,1536]{1,0:T(8,128)(2,1)} %get-tuple-element.8) | copy-start | bytes 589828
